TPU v7x, 256 devices: a whole 4x4x8 slice. The times are simulated.
256 devices in a mesh: ctx: 32 (over z, x), tp: 8 (over y, core).
Axes of the slice: x: 4, y: 4, z: 8, core: 2. Of those that a mesh axis runs over, the one named last changes fastest.
Arguments:
- query_in: bfloat16 [16384, 8192], P('ctx', 'tp'), may hold values from -6 to 6
- key_in: bfloat16 [16384, 8192], P('ctx', 'tp'), may hold values from -6 to 6
- value_in: bfloat16 [16384, 8192], P('ctx', 'tp'), may hold values from -6 to 6
- filters: bfloat16 [512, 128], P('tp'), may hold values from -0.5 to 0.5
- proj_out: bfloat16 [4096, 8192], P('ctx', 'tp'), may hold values from -0.0625 to 0.0625
- cotangent: bfloat16 [16384, 4096], P('ctx', 'tp'), may hold values from -6 to 6
Outputs:
- grad_query: bfloat16 [16384, 8192], P('ctx', 'tp')
- grad_key: bfloat16 [16384, 8192], P('ctx', 'tp')
- grad_value: bfloat16 [16384, 8192], P('ctx', 'tp')
- grad_filter: float32 [512, 128], P('tp')
- grad_proj: float32 [4096, 8192], P('ctx', 'tp')
All inputs are finite; a program needn't handle non-finite values.
Results may differ from a plain program's by a relative error of at most 0.005.
Values may be sent and summed in bfloat16 or wider, within the bound.
No kernel may reach another device: no remote copies, remote signals or barrier semaphores. Data moves between devices by JAX's collectives and lax.ppermute only.
A program may use at most 192 MiB of HBM per device.

v0:
```python
import jax
import jax.numpy as jnp
from jax import lax
from jax.sharding import PartitionSpec as P


def from_behind(value, axis, by):
    count = lax.axis_size(axis)
    pairs = [(i, i + by) for i in range(count) if 0 <= i + by < count]
    return lax.ppermute(value, axis, pairs)


def toeplitz_rows(filters):
    group_count, tap_count = filters.shape
    padded = jnp.concatenate(
        [
            jnp.zeros((group_count, 1), filters.dtype),
            jnp.flip(filters, 1),
            jnp.zeros((group_count, 2 * tap_count - 1), filters.dtype),
        ],
        1,
    )
    tiled = jnp.tile(padded, (1, tap_count))[:, : tap_count * (3 * tap_count - 1)]
    return tiled.reshape(group_count, tap_count, 3 * tap_count - 1)[:, :, : 2 * tap_count]


def on_device(query_in, key_in, value_in, filters, proj_out, cotangent):
    tok_rows, chan_width = query_in.shape
    group_count, tap_count = filters.shape
    group_size = chan_width // group_count
    blocks = tok_rows // tap_count
    table = toeplitz_rows(filters)
    mixed_in = (key_in.astype(jnp.float32) * value_in.astype(jnp.float32)).astype(jnp.bfloat16)
    left_rim = from_behind(mixed_in[tok_rows - tap_count + 1 :], "ctx", 1)
    extended = jnp.concatenate(
        [jnp.zeros((1, chan_width), jnp.bfloat16), left_rim, mixed_in[: tok_rows - tap_count]], 0
    )
    window = jnp.concatenate(
        [
            extended.reshape(blocks, tap_count, group_count, group_size),
            mixed_in.reshape(blocks, tap_count, group_count, group_size),
        ],
        1,
    )
    conv_out = jnp.einsum(
        "gts,bsgc->btgc", table, window, preferred_element_type=jnp.float32
    ).reshape(tok_rows, chan_width)
    gated = (query_in.astype(jnp.float32) * conv_out).astype(jnp.bfloat16)
    cot_full = lax.all_gather(cotangent, "tp", axis=1, tiled=True)
    columns = cot_full
    grad_all = jnp.dot(
        columns,
        lax.all_gather(proj_out, "ctx", axis=0, tiled=True),
        preferred_element_type=jnp.float32,
    )
    grad_query = (grad_all * conv_out).astype(jnp.bfloat16)
    grad_inner = (grad_all * query_in.astype(jnp.float32)).astype(jnp.bfloat16)
    next_rows = from_behind(grad_inner[: tap_count - 1], "ctx", -1)
    ahead = jnp.concatenate(
        [grad_inner[tap_count:], next_rows, jnp.zeros((1, chan_width), jnp.bfloat16)], 0
    )
    inner_blocks = grad_inner.reshape(blocks, tap_count, group_count, group_size)
    ahead_blocks = ahead.reshape(blocks, tap_count, group_count, group_size)
    grad_mixed = jnp.einsum(
        "gts,btgc->bsgc", table[:, :, tap_count:], inner_blocks, preferred_element_type=jnp.float32
    )
    grad_mixed = grad_mixed + jnp.einsum(
        "gts,btgc->bsgc", table[:, :, :tap_count], ahead_blocks, preferred_element_type=jnp.float32
    )
    grad_mixed = grad_mixed.reshape(tok_rows, chan_width)
    grad_key = (grad_mixed * value_in.astype(jnp.float32)).astype(jnp.bfloat16)
    grad_value = (grad_mixed * key_in.astype(jnp.float32)).astype(jnp.bfloat16)
    corr = jnp.einsum("btgc,bsgc->gts", inner_blocks, window, preferred_element_type=jnp.float32)
    skewed = jnp.pad(corr.reshape(group_count, -1), ((0, 0), (0, tap_count))).reshape(
        group_count, tap_count, 2 * tap_count + 1
    )
    filter_part = jnp.flip(jnp.sum(skewed, axis=1)[:, 1 : tap_count + 1], 1)
    columns = cot_full
    grad_proj = lax.psum_scatter(
        lax.dot_general(
            columns, gated, (((0,), (0,)), ((), ())), preferred_element_type=jnp.float32
        ),
        "ctx",
        scatter_dimension=0,
        tiled=True,
    )
    grad_filter = lax.psum(filter_part, "ctx")
    return (grad_query, grad_key, grad_value, grad_filter, grad_proj)


def solution(mesh):
    placed = (
        P("ctx", "tp"),
        P("ctx", "tp"),
        P("ctx", "tp"),
        P("tp", None),
        P("ctx", "tp"),
        P("ctx", "tp"),
    )
    return jax.shard_map(
        on_device,
        mesh=mesh,
        in_specs=placed,
        out_specs=(P("ctx", "tp"), P("ctx", "tp"), P("ctx", "tp"), P("tp", None), P("ctx", "tp")),
        check_vma=False,
    )
```

profile of v0, /device:TPU:8, one launch (start us, length us, event | category | flops | bytes accessed | tf_op | source)
XLA Modules:
  0.0 496.2 jit_solution(13362791816464786184)
XLA Ops:
  7.2 0.0 all-gather.3.cloned.1.call-start
  7.2 0.7 all-gather.3.cloned.1.call-update
  7.9 0.0 all-gather.5.cloned.1.call-start
  7.9 0.7 all-gather.5.cloned.1.call-update
  8.6 0.0 copy-start.3
  8.7 0.0 copy-start.2
  8.7 0.0 reduce-scatter.2.cloned.1.call-start
  8.7 37.7 %all-gather.3.cloned.1.call-done = bf16[512,4096]{1,0:T(8,128)(2,1)} async-done(((bf16[512,512]{1,0:T(8,128)(2,1)}), bf16[512,4096]{1,0:T(8,128)(2,1)}) %all-gather.3.cloned.1.call-update) | async-done | bytes 4194320 | tf_op jit(solution)/shard_map/all_gather | solution.py:49
  46.4 101.9 %all-gather.5.cloned.1.call-done = bf16[4096,1024]{1,0:T(8,128)(2,1)} async-done(((bf16[128,1024]{1,0:T(8,128)(2,1)}), bf16[4096,1024]{1,0:T(8,128)(2,1)}) %all-gather.5.cloned.1.call-update) | async-done | bytes 8388624 | tf_op jit(solution)/shard_map/all_gather | solution.py:53
  148.3 10.6 %fusion.4 = (bf16[512,1024]{1,0:T(8,128)(2,1)S(1)}, f32[512,1024]{1,0:T(8,128)}) fusion(bf16[512,1024]{1,0:T(8,128)(2,1)} %param.6, bf16[512,4096]{1,0:T(8,128)(2,1)} %all-gather.3.cloned.1.call-done, bf16[4096,1024]{1,0:T(8,128)(2,1)} %all-gather.5.cloned.1.call-done), kind=kOutput, calls=%fused_computation.11 | convolution fusion | flops 4296540160 | bytes 16777216 | tf_op jit(solution)/shard_map/dot_general | solution.py:51
  159.0 1.5 collective-permute-start.1
  160.4 0.1 pad.7.clone
  160.5 0.1 pad.10.clone
  160.6 0.0 copy-done.3
  160.6 0.1 rev.8
  160.7 0.0 copy-done.2
  160.7 0.5 copy.16
  161.2 2.3 copy.17
  163.5 0.1 maximum_maximum_fusion.1
  163.6 0.5 tile.4
  164.2 4.1 copy.37
  168.2 3.1 slice.40
  171.3 16.4 %reshape.43 = bf16[64,128,383]{2,1,0:T(8,128)(2,1)} reshape(bf16[64,49024]{1,0:T(8,128)(2,1)} %slice.40) | data formatting | bytes 12550144 | tf_op jit(solution)/shard_map/reshape | solution.py:24
  187.7 0.9 slice.43
  188.7 1.3 copy.23
  190.0 1.3 reshape.45
  191.3 0.0 collective-permute-done.1
  191.3 1.5 maximum_maximum_fusion
  192.8 1.3 copy.25
  194.1 1.3 reshape.46
  195.5 2.3 fusion.6
  197.7 2.3 add_bitcast_fusion
  200.0 0.0 copy-start.1
  200.1 1.0 copy.27
  201.0 0.2 copy-done.1
  201.3 2.0 fusion.1
  203.2 0.1 slice.38
  203.4 5.3 %collective-permute-start = (bf16[127,1024]{0,1:T(8,128)(2,1)S(1)}, bf16[127,1024]{0,1:T(8,128)(2,1)}, u32[]{:S(2)}, u32[]{:S(2)}) collective-permute-start(bf16[127,1024]{0,1:T(8,128)(2,1)S(1)} %slice.38), channel_id=1, source_target_pairs={{0,8},{8,16},{16,24},{24,32},{32,40},{40,48},{48,56},{56,64},{64,7... | collective-permute-start | bytes 780296 | tf_op jit(solution)/shard_map/ppermute | solution.py:10
  208.7 1.0 slice.39
  209.6 0.3 reshape.42
  209.9 2.9 collective-permute-done
  212.8 2.5 pad_maximum_fusion
  215.3 1.3 reshape.41
  216.6 0.3 copy_dynamic-update-slice_fusion.1
  216.9 0.4 copy_dynamic-update-slice_fusion
  217.3 4.5 fusion.8
  221.9 1.0 copy.21
  222.8 1.5 copy.52
  224.4 1.9 copy.22
  226.3 12.8 %convolution_bitcast_fusion = f32[4096,1024]{0,1:T(8,128)} fusion(bf16[512,4096]{1,0:T(8,128)(2,1)} %all-gather.3.cloned.1.call-done, f32[512,1024]{1,0:T(8,128)S(1)} %copy.22, bf16[512,1024]{1,0:T(8,128)(2,1)} %param.6), kind=kOutput, calls=%fused_computation | convolution fusion | flops 4296540160 | bytes 24117248 | tf_op jit(solution)/shard_map/dot_general | solution.py:80
  239.1 0.0 reduce-scatter.2.cloned.1.call-update
  239.1 2.3 copy.31
  241.4 2.3 copy.30
  243.7 2.9 fusion.11
  246.6 4.7 copy.40
  251.3 3.9 pad.4
  255.2 14.2 %reshape.49 = f32[64,128,257]{2,1,0:T(8,128)} reshape(f32[64,32896]{1,0:T(8,128)} %pad.4) | data formatting | bytes 16842752 | tf_op jit(solution)/shard_map/reshape | solution.py:74
  269.4 6.2 %reduce_sum.9 = f32[64,257]{1,0:T(8,128)S(1)} reduce(f32[64,128,257]{2,1,0:T(8,128)} %reshape.49, f32[]{:T(128)} %constant.3.clone.1), dimensions={1}, to_apply=%region_0.1 | reduce | flops 2088896 | bytes 8487172 | tf_op jit(solution)/shard_map/reduce_sum | solution.py:77
  275.6 0.1 slice.46
  275.7 0.1 rev.9
  275.8 143.0 %psum.7 = f32[64,128]{1,0:T(8,128)} all-reduce(f32[64,128]{1,0:T(8,128)S(1)} %rev.9), channel_id=1, replica_groups=mesh['ctx'=32,'tp'=8] {'ctx'}, use_global_device_ids=true, to_apply=%region_1.2 | all-reduce | flops 8192 | bytes 65536 | tf_op jit(solution)/shard_map/psum | solution.py:87
  418.7 2.9 multiply_convert_fusion
  421.6 66.0 %reduce-scatter.2.cloned.1.call-done = f32[128,1024]{0,1:T(8,128)} async-done(((f32[4096,1024]{0,1:T(8,128)}), f32[128,1024]{0,1:T(8,128)}) %reduce-scatter.2.cloned.1.call-update) | async-done | bytes 524304 | tf_op jit(solution)/shard_map/reduce_scatter | solution.py:79
  487.7 2.0 copy.32
  (6 shorter events, 0.0 us)
Async XLA Ops:
  7.2 39.2 %all-gather.3.cloned.1.call-start = ((), (), s32[]{:S(2)}) async-start(), calls=%async_computation.1 | async-start | bytes 4718592 | tf_op jit(solution)/shard_map/all_gather | solution.py:49
  7.9 140.4 %all-gather.5.cloned.1.call-start = ((), (), s32[]{:S(2)}) async-start(), calls=%async_computation.2 | async-start | bytes 8650752 | tf_op jit(solution)/shard_map/all_gather | solution.py:53
  8.6 152.0 %copy-start.3 = (bf16[64,128]{1,0:T(8,128)(2,1)S(1)}, bf16[64,128]{1,0:T(8,128)(2,1)}, u32[]{:S(2)}) copy-start(bf16[64,128]{1,0:T(8,128)(2,1)} %param.9) | copy-start | bytes 49156
  8.7 152.0 %copy-start.2 = (bf16[512,1024]{1,0:T(8,128)(2,1)S(1)}, bf16[512,1024]{1,0:T(8,128)(2,1)}, u32[]{:S(2)}) copy-start(bf16[512,1024]{1,0:T(8,128)(2,1)} %param.7) | copy-start | bytes 3145732
  8.7 479.0 %reduce-scatter.2.cloned.1.call-start = ((), (), s32[]{:S(2)}) async-start(), calls=%async_computation.3 | async-start | bytes 17301504 | tf_op jit(solution)/shard_map/reduce_scatter | solution.py:79
  159.0 32.4 %collective-permute-start.1 = (bf16[127,1024]{1,0:T(8,128)(2,1)S(1)}, bf16[127,1024]{1,0:T(8,128)(2,1)}, u32[]{:S(2)}, u32[]{:S(2)}) collective-permute-start(bf16[127,1024]{1,0:T(8,128)(2,1)S(1)} %slice.44), channel_id=1, source_target_pairs={{8,0},{16,8},{24,16},{32,24},{40,32},{48,40},{56,48},{64,56},{72,6... | collective-permute-start | bytes 780296 | tf_op jit(solution)/shard_map/ppermute | solution.py:10
  200.0 1.2 copy-start.1
  203.4 9.4 %collective-permute-start = (bf16[127,1024]{0,1:T(8,128)(2,1)S(1)}, bf16[127,1024]{0,1:T(8,128)(2,1)}, u32[]{:S(2)}, u32[]{:S(2)}) collective-permute-start(bf16[127,1024]{0,1:T(8,128)(2,1)S(1)} %slice.38), channel_id=1, source_target_pairs={{0,8},{8,16},{16,24},{24,32},{32,40},{40,48},{48,56},{56,64},{64,7... | collective-permute-start | bytes 780296 | tf_op jit(solution)/shard_map/ppermute | solution.py:10
  217.3 4.5 copy-start
Sparse Core Ops, SparseCore 0:
  9.8 36.5 all-gather.2
  49.0 99.3 all-gather.4
  239.3 248.3 reduce-scatter.1
where the time goes:
time: 497 us; the launch traced here: 496 us
  waiting for transfers between devices  210 us (42%)
  blocking collectives  143 us (29%)
  local copies, waits for them, and re-layouts  72 us (14%)
  matrix products  35.4 us (7%)
  other arithmetic  15.1 us (3%)
  between operations  14 us (3%)
  starting transfers between devices  6.87 us (1%)
    psum x1, blocking collectives, on_device(): grad_filter = lax.psum(filter_part, 'ctx')  143 us
    all_gather x1, waiting for transfers between devices, on_device(): lax.all_gather(proj_out, 'ctx', axis=0, tiled=True)  102 us
    reduce_scatter x1, waiting for transfers between devices, on_device(): lax.psum_scatter(lax.dot_general(columns, gated, (((0,), (0,)), ((), ()))...  66 us
    all_gather x1, waiting for transfers between devices, on_device(): cot_full = lax.all_gather(cotangent, 'tp', axis=1, tiled=True)  37.7 us
    unnamed x17, local copies, waits for them, and re-layouts  20.2 us
    reshape x1, local copies, waits for them, and re-layouts, toeplitz_rows(): tiled.reshape(group_count, tap_count, 3 * tap_count - 1)  16.4 us
    reshape x1, local copies, waits for them, and re-layouts, on_device(): jnp.pad(corr.reshape(group_count, -1), ((0, 0), (0, tap_count)))  14.2 us
    dot_general x1, matrix products, on_device(): lax.dot_general(columns, gated, (((0,), (0,)), ((), ())), preferred_eleme...  12.8 us
  transfers between devices with their start and end apart: 5, of which 4 were waited for; matrix products, arithmetic and copies ran while one was open for 14% of the time, Pallas kernels for 0%

commit v1 on v0

--- a/solution.py
+++ b/solution.py
@@ -46,7 +46,12 @@
         "gts,bsgc->btgc", table, window, preferred_element_type=jnp.float32
     ).reshape(tok_rows, chan_width)
     gated = (query_in.astype(jnp.float32) * conv_out).astype(jnp.bfloat16)
-    cot_full = lax.all_gather(cotangent, "tp", axis=1, tiled=True)
+    ring = [cotangent]
+    for hop in range(7):
+        ring.append(lax.ppermute(ring[-1], "tp", [(dev, (dev + 1) % 8) for dev in range(8)]))
+    cot_full = jnp.roll(
+        jnp.concatenate(ring[::-1], axis=1), (lax.axis_index("tp") + 1) * ring[0].shape[1], axis=1
+    )
     columns = cot_full
     grad_all = jnp.dot(
         columns,

time: 497 us -> 460 us (0.926)
  waiting for transfers between devices: 210 us -> 157 us
  local copies, waits for them, and re-layouts: 72 us -> 91.6 us
    all_gather x1, waiting for transfers between devices: 102 us -> 24.6 us  [on_device(): lax.all_gather(proj_out, 'ctx', axis=0, tiled=True)]
    ppermute x0 -> x7, waiting for transfers between devices: none -> 60.8 us  [on_device(): lax.ppermute(ring[-1], 'tp', [(dev, (dev + 1) % 8) for dev in range(8)])]
    all_gather x1 -> x0, waiting for transfers between devices: 37.7 us -> none  [on_device(): cot_full = lax.all_gather(cotangent, 'tp', axis=1, tiled=True)]
    unnamed x17 -> x33, local copies, waits for them, and re-layouts: 20.2 us -> 36.7 us
  transfers between devices with their start and end apart: 5 -> 11, of which waited for: 4 -> 10; matrix products, arithmetic and copies ran while one was open for 14% -> 19% of each run, Pallas kernels for 0% -> 0%
where the time goes in v1:
time: 460 us; the launch traced here: 459 us
  waiting for transfers between devices  157 us (34%)
  blocking collectives  142 us (31%)
  local copies, waits for them, and re-layouts  91.6 us (20%)
  matrix products  33.7 us (7%)
  between operations  14.3 us (3%)
  other arithmetic  13.1 us (3%)
  starting transfers between devices  6.37 us (1%)
    psum x1, blocking collectives, on_device(): grad_filter = lax.psum(filter_part, 'ctx')  142 us
    reduce_scatter x1, waiting for transfers between devices, on_device(): lax.psum_scatter(lax.dot_general(columns, gated, (((0,), (0,)), ((), ()))...  67.7 us
    ppermute x7, waiting for transfers between devices, on_device(): lax.ppermute(ring[-1], 'tp', [(dev, (dev + 1) % 8) for dev in range(8)])  60.8 us
    unnamed x33, local copies, waits for them, and re-layouts  36.7 us
    all_gather x1, waiting for transfers between devices, on_device(): lax.all_gather(proj_out, 'ctx', axis=0, tiled=True)  24.6 us
    reshape x1, local copies, waits for them, and re-layouts, toeplitz_rows(): tiled.reshape(group_count, tap_count, 3 * tap_count - 1)  16.5 us
    reshape x1, local copies, waits for them, and re-layouts, on_device(): jnp.pad(corr.reshape(group_count, -1), ((0, 0), (0, tap_count)))  14.4 us
    dot_general x1, matrix products, on_device(): lax.dot_general(columns, gated, (((0,), (0,)), ((), ())), preferred_eleme...  13.4 us
  transfers between devices with their start and end apart: 11, of which 10 were waited for; matrix products, arithmetic and copies ran while one was open for 19% of the time, Pallas kernels for 0%

profile of v1, /device:TPU:8, one launch (start us, length us, event | category | flops | bytes accessed | tf_op | source)
XLA Modules:
  0.0 458.5 jit_solution(15108991487471855924)
XLA Ops:
  7.2 0.7 all-gather.2.cloned.1.call-update
  8.0 8.8 %collective-permute-done = bf16[512,512]{1,0:T(8,128)(2,1)S(1)} collective-permute-done((bf16[512,512]{1,0:T(8,128)(2,1)}, bf16[512,512]{1,0:T(8,128)(2,1)S(1)}, u32[]{:S(2)}, u32[]{:S(2)}) %collective-permute-start) | collective-permute-done | bytes 524320 | tf_op jit(solution)/shard_map/ppermute | solution.py:51
  16.8 8.6 %collective-permute-done.1 = bf16[512,512]{1,0:T(8,128)(2,1)S(1)} collective-permute-done((bf16[512,512]{1,0:T(8,128)(2,1)S(1)}, bf16[512,512]{1,0:T(8,128)(2,1)S(1)}, u32[]{:S(2)}, u32[]{:S(2)}) %collective-permute-start.1) | collective-permute-done | bytes 524320 | tf_op jit(solution)/shard_map/ppermute | solution.py:51
  25.4 8.6 %collective-permute-done.2 = bf16[512,512]{1,0:T(8,128)(2,1)S(1)} collective-permute-done((bf16[512,512]{1,0:T(8,128)(2,1)S(1)}, bf16[512,512]{1,0:T(8,128)(2,1)S(1)}, u32[]{:S(2)}, u32[]{:S(2)}) %collective-permute-start.2) | collective-permute-done | bytes 524320 | tf_op jit(solution)/shard_map/ppermute | solution.py:51
  34.0 8.6 %collective-permute-done.3 = bf16[512,512]{1,0:T(8,128)(2,1)S(1)} collective-permute-done((bf16[512,512]{1,0:T(8,128)(2,1)S(1)}, bf16[512,512]{1,0:T(8,128)(2,1)S(1)}, u32[]{:S(2)}, u32[]{:S(2)}) %collective-permute-start.3) | collective-permute-done | bytes 524320 | tf_op jit(solution)/shard_map/ppermute | solution.py:51
  42.6 8.6 %collective-permute-done.4 = bf16[512,512]{1,0:T(8,128)(2,1)S(1)} collective-permute-done((bf16[512,512]{1,0:T(8,128)(2,1)S(1)}, bf16[512,512]{1,0:T(8,128)(2,1)S(1)}, u32[]{:S(2)}, u32[]{:S(2)}) %collective-permute-start.4) | collective-permute-done | bytes 524320 | tf_op jit(solution)/shard_map/ppermute | solution.py:51
  51.2 8.7 %collective-permute-done.5 = bf16[512,512]{1,0:T(8,128)(2,1)} collective-permute-done((bf16[512,512]{1,0:T(8,128)(2,1)S(1)}, bf16[512,512]{1,0:T(8,128)(2,1)}, u32[]{:S(2)}, u32[]{:S(2)}) %collective-permute-start.5) | collective-permute-done | bytes 524320 | tf_op jit(solution)/shard_map/ppermute | solution.py:51
  59.9 8.9 %collective-permute-done.6 = bf16[512,512]{1,0:T(8,128)(2,1)} collective-permute-done((bf16[512,512]{1,0:T(8,128)(2,1)}, bf16[512,512]{1,0:T(8,128)(2,1)}, u32[]{:S(2)}, u32[]{:S(2)}) %collective-permute-start.6) | collective-permute-done | bytes 524320 | tf_op jit(solution)/shard_map/ppermute | solution.py:51
  68.8 1.9 constant_dynamic-update-slice_fusion.15
  70.8 1.9 constant_dynamic-update-slice_fusion.14
  72.7 0.9 constant_dynamic-update-slice_fusion.13
  73.6 0.9 constant_dynamic-update-slice_fusion.12
  74.5 0.9 constant_dynamic-update-slice_fusion.11
  75.4 0.9 constant_dynamic-update-slice_fusion.10
  76.3 0.9 constant_dynamic-update-slice_fusion.9
  77.2 1.0 constant_dynamic-update-slice_fusion.8
  78.2 1.9 constant_dynamic-update-slice_fusion.7
  80.1 2.0 constant_dynamic-update-slice_fusion.6
  82.1 0.9 constant_dynamic-update-slice_fusion.5
  83.0 0.9 constant_dynamic-update-slice_fusion.4
  83.8 0.8 constant_dynamic-update-slice_fusion.3
  84.7 0.8 constant_dynamic-update-slice_fusion.2
  85.5 0.9 constant_dynamic-update-slice_fusion.1
  86.4 0.8 constant_dynamic-update-slice_fusion
  87.3 24.6 %all-gather.2.cloned.1.call-done = bf16[4096,1024]{1,0:T(8,128)(2,1)} async-done(((bf16[128,1024]{1,0:T(8,128)(2,1)}), bf16[4096,1024]{1,0:T(8,128)(2,1)}) %all-gather.2.cloned.1.call-update) | async-done | bytes 8388624 | tf_op jit(solution)/shard_map/all_gather | solution.py:58
  111.8 10.6 %fusion.8 = (bf16[512,1024]{1,0:T(8,128)(2,1)S(1)}, f32[512,1024]{1,0:T(8,128)}) fusion(bf16[512,1024]{1,0:T(8,128)(2,1)} %param.6, bf16[4096,1024]{1,0:T(8,128)(2,1)} %all-gather.2.cloned.1.call-done, bf16[512,8192]{1,0:T(8,128)(2,1)} %constant_dynamic-update-slice_fusion, s32[]{:T(128)S(6)} %select_n.14), kind=kOutput, calls=%fused_computation.14 | convolution fusion | flops 4296540160 | bytes 16777220 | tf_op jit(solution)/shard_map/dot_general | solution.py:56
  122.5 1.5 collective-permute-start.8
  124.3 0.5 tile.4
  124.8 4.1 copy.35
  128.9 3.1 slice.40
  132.0 16.5 %reshape.43 = bf16[64,128,383]{2,1,0:T(8,128)(2,1)} reshape(bf16[64,49024]{1,0:T(8,128)(2,1)} %slice.40) | data formatting | bytes 12550144 | tf_op jit(solution)/shard_map/reshape | solution.py:24
  148.5 0.5 copy.15
  149.0 2.3 copy.16
  151.3 0.9 slice.43
  152.2 1.3 copy.22
  153.6 1.3 reshape.45
  154.9 1.5 maximum_maximum_fusion
  156.4 1.3 copy.24
  157.7 1.3 reshape.46
  159.1 2.3 fusion.10
  161.3 2.4 add_bitcast_fusion
  163.7 1.0 copy.26
  164.7 2.0 fusion.5
  166.8 4.8 %collective-permute-start.7 = (bf16[127,1024]{0,1:T(8,128)(2,1)S(1)}, bf16[127,1024]{0,1:T(8,128)(2,1)S(1)}, u32[]{:S(2)}, u32[]{:S(2)}) collective-permute-start(bf16[127,1024]{0,1:T(8,128)(2,1)S(1)} %slice.38), channel_id=1, source_target_pairs={{0,8},{8,16},{16,24},{24,32},{32,40},{40,48},{48,56},{56,64},{64,7... | collective-permute-start | bytes 780296 | tf_op jit(solution)/shard_map/ppermute | solution.py:10
  171.7 1.1 reshape.42
  172.9 3.4 collective-permute-done.7
  176.6 1.1 reshape.41
  177.7 1.5 copy_dynamic-update-slice_fusion.1
  179.2 1.7 copy_dynamic-update-slice_fusion
  180.9 3.7 fusion.12
  184.6 1.0 copy.20
  185.6 1.5 copy.50
  187.1 2.9 copy.21
  190.0 13.4 %fusion.1 = f32[4096,1024]{1,0:T(8,128)} fusion(bf16[512,8192]{1,0:T(8,128)(2,1)} %constant_dynamic-update-slice_fusion, s32[]{:T(128)S(6)} %select_n.14, f32[512,1024]{1,0:T(8,128)} %copy.21, bf16[512,1024]{1,0:T(8,128)(2,1)} %param.6), kind=kOutput, calls=%fused_computation.2 | convolution fusion | flops 4296540160 | bytes 24117252 | tf_op jit(solution)/shard_map/dot_general | solution.py:85
  203.5 2.3 copy.29
  205.7 2.3 copy.30
  208.0 1.3 fusion.15
  209.3 4.7 %copy.38 = f32[8,8,128,256]{3,1,2,0:T(8,128)S(1)} copy(f32[8,8,128,256]{3,2,1,0:T(8,128)S(1)} %bitcast.58) | data formatting | bytes 16777216
  214.0 3.9 pad.4
  217.9 14.4 %reshape.49 = f32[64,128,257]{2,1,0:T(8,128)} reshape(f32[64,32896]{1,0:T(8,128)} %pad.4) | data formatting | bytes 16842752 | tf_op jit(solution)/shard_map/reshape | solution.py:79
  232.3 6.4 %reduce_sum.9 = f32[64,257]{1,0:T(8,128)S(1)} reduce(f32[64,128,257]{2,1,0:T(8,128)} %reshape.49, f32[]{:T(128)} %constant.37.clone.1), dimensions={1}, to_apply=%region_0.1 | reduce | flops 2088896 | bytes 8487172 | tf_op jit(solution)/shard_map/reduce_sum | solution.py:82
  238.8 142.2 %psum.7 = f32[64,128]{1,0:T(8,128)} all-reduce(f32[64,128]{1,0:T(8,128)S(1)} %rev.9), channel_id=1, replica_groups=mesh['ctx'=32,'tp'=8] {'ctx'}, use_global_device_ids=true, to_apply=%region_1.2 | all-reduce | flops 8192 | bytes 65536 | tf_op jit(solution)/shard_map/psum | solution.py:92
  381.1 2.9 multiply_convert_fusion
  384.0 67.7 %reduce-scatter.2.cloned.1.call-done = f32[128,1024]{1,0:T(8,128)} async-done(((f32[4096,1024]{1,0:T(8,128)}), f32[128,1024]{1,0:T(8,128)}) %reduce-scatter.2.cloned.1.call-update) | async-done | bytes 524304 | tf_op jit(solution)/shard_map/reduce_scatter | solution.py:84
  (34 shorter events, 1.2 us)
Async XLA Ops:
  7.2 70.0 %copy-start.2 = (bf16[512,512]{1,0:T(8,128)(2,1)S(1)}, bf16[512,512]{1,0:T(8,128)(2,1)}, u32[]{:S(2)}) copy-start(bf16[512,512]{1,0:T(8,128)(2,1)} %param.11) | copy-start | bytes 1572868
  7.2 104.6 %all-gather.2.cloned.1.call-start = ((), (), s32[]{:S(2)}) async-start(), calls=%async_computation.1 | async-start | bytes 8650752 | tf_op jit(solution)/shard_map/all_gather | solution.py:58
  7.9 443.8 %reduce-scatter.2.cloned.1.call-start = ((), (), s32[]{:S(2)}) async-start(), calls=%async_computation.2 | async-start | bytes 17301504 | tf_op jit(solution)/shard_map/reduce_scatter | solution.py:84
  8.0 8.8 %collective-permute-start = (bf16[512,512]{1,0:T(8,128)(2,1)}, bf16[512,512]{1,0:T(8,128)(2,1)S(1)}, u32[]{:S(2)}, u32[]{:S(2)}) collective-permute-start(bf16[512,512]{1,0:T(8,128)(2,1)} %param.11), channel_id=1, source_target_pairs={{0,1},{1,2},{2,3},{3,4},{4,5},{5,6},{6,7},{7,0},{8,9},{9,10},{10,1... | collective-permute-start | bytes 1572872 | tf_op jit(solution)/shard_map/ppermute | solution.py:51
  16.8 8.6 %collective-permute-start.1 = (bf16[512,512]{1,0:T(8,128)(2,1)S(1)}, bf16[512,512]{1,0:T(8,128)(2,1)S(1)}, u32[]{:S(2)}, u32[]{:S(2)}) collective-permute-start(bf16[512,512]{1,0:T(8,128)(2,1)S(1)} %collective-permute-done), channel_id=1, source_target_pairs={{0,1},{1,2},{2,3},{3,4},{4,5},{5,6},{6,7},{7,0},{8,9},{9,10},{10,1... | collective-permute-start | bytes 1572872 | tf_op jit(solution)/shard_map/ppermute | solution.py:51
  25.4 8.6 %collective-permute-start.2 = (bf16[512,512]{1,0:T(8,128)(2,1)S(1)}, bf16[512,512]{1,0:T(8,128)(2,1)S(1)}, u32[]{:S(2)}, u32[]{:S(2)}) collective-permute-start(bf16[512,512]{1,0:T(8,128)(2,1)S(1)} %collective-permute-done.1), channel_id=1, source_target_pairs={{0,1},{1,2},{2,3},{3,4},{4,5},{5,6},{6,7},{7,0},{8,9},{9,10},{10,1... | collective-permute-start | bytes 1572872 | tf_op jit(solution)/shard_map/ppermute | solution.py:51
  34.0 8.6 %collective-permute-start.3 = (bf16[512,512]{1,0:T(8,128)(2,1)S(1)}, bf16[512,512]{1,0:T(8,128)(2,1)S(1)}, u32[]{:S(2)}, u32[]{:S(2)}) collective-permute-start(bf16[512,512]{1,0:T(8,128)(2,1)S(1)} %collective-permute-done.2), channel_id=1, source_target_pairs={{0,1},{1,2},{2,3},{3,4},{4,5},{5,6},{6,7},{7,0},{8,9},{9,10},{10,1... | collective-permute-start | bytes 1572872 | tf_op jit(solution)/shard_map/ppermute | solution.py:51
  42.6 8.6 %collective-permute-start.4 = (bf16[512,512]{1,0:T(8,128)(2,1)S(1)}, bf16[512,512]{1,0:T(8,128)(2,1)S(1)}, u32[]{:S(2)}, u32[]{:S(2)}) collective-permute-start(bf16[512,512]{1,0:T(8,128)(2,1)S(1)} %collective-permute-done.3), channel_id=1, source_target_pairs={{0,1},{1,2},{2,3},{3,4},{4,5},{5,6},{6,7},{7,0},{8,9},{9,10},{10,1... | collective-permute-start | bytes 1572872 | tf_op jit(solution)/shard_map/ppermute | solution.py:51
  51.2 8.7 %collective-permute-start.5 = (bf16[512,512]{1,0:T(8,128)(2,1)S(1)}, bf16[512,512]{1,0:T(8,128)(2,1)}, u32[]{:S(2)}, u32[]{:S(2)}) collective-permute-start(bf16[512,512]{1,0:T(8,128)(2,1)S(1)} %collective-permute-done.4), channel_id=1, source_target_pairs={{0,1},{1,2},{2,3},{3,4},{4,5},{5,6},{6,7},{7,0},{8,9},{9,10},{10,1... | collective-permute-start | bytes 1572872 | tf_op jit(solution)/shard_map/ppermute | solution.py:51
  59.9 8.9 %collective-permute-start.6 = (bf16[512,512]{1,0:T(8,128)(2,1)}, bf16[512,512]{1,0:T(8,128)(2,1)}, u32[]{:S(2)}, u32[]{:S(2)}) collective-permute-start(bf16[512,512]{1,0:T(8,128)(2,1)} %collective-permute-done.5), channel_id=1, source_target_pairs={{0,1},{1,2},{2,3},{3,4},{4,5},{5,6},{6,7},{7,0},{8,9},{9,10},{10,1... | collective-permute-start | bytes 1572872 | tf_op jit(solution)/shard_map/ppermute | solution.py:51
  87.2 36.8 %copy-start.4 = (bf16[64,128]{1,0:T(8,128)(2,1)S(1)}, bf16[64,128]{1,0:T(8,128)(2,1)}, u32[]{:S(2)}) copy-start(bf16[64,128]{1,0:T(8,128)(2,1)} %param.9) | copy-start | bytes 49156
  122.5 32.5 %collective-permute-start.8 = (bf16[127,1024]{1,0:T(8,128)(2,1)S(1)}, bf16[127,1024]{1,0:T(8,128)(2,1)}, u32[]{:S(2)}, u32[]{:S(2)}) collective-permute-start(bf16[127,1024]{1,0:T(8,128)(2,1)S(1)} %slice.44), channel_id=1, source_target_pairs={{8,0},{16,8},{24,16},{32,24},{40,32},{48,40},{56,48},{64,56},{72,6... | collective-permute-start | bytes 780296 | tf_op jit(solution)/shard_map/ppermute | solution.py:10
  132.0 16.5 %copy-start.3 = (bf16[512,1024]{1,0:T(8,128)(2,1)S(1)}, bf16[512,1024]{1,0:T(8,128)(2,1)}, u32[]{:S(2)}) copy-start(bf16[512,1024]{1,0:T(8,128)(2,1)} %param.7) | copy-start | bytes 3145732
  161.3 3.4 copy-start.1
  166.8 9.4 %collective-permute-start.7 = (bf16[127,1024]{0,1:T(8,128)(2,1)S(1)}, bf16[127,1024]{0,1:T(8,128)(2,1)S(1)}, u32[]{:S(2)}, u32[]{:S(2)}) collective-permute-start(bf16[127,1024]{0,1:T(8,128)(2,1)S(1)} %slice.38), channel_id=1, source_target_pairs={{0,8},{8,16},{16,24},{24,32},{32,40},{40,48},{48,56},{56,64},{64,7... | collective-permute-start | bytes 780296 | tf_op jit(solution)/shard_map/ppermute | solution.py:10
  232.3 148.8 %copy-start = (f32[512,1024]{1,0:T(8,128)S(1)}, f32[512,1024]{1,0:T(8,128)}, u32[]{:S(2)}) copy-start(f32[512,1024]{1,0:T(8,128)} %copy.21) | copy-start | bytes 6291460
Sparse Core Ops, SparseCore 0:
  10.6 101.1 all-gather.1
  203.6 248.0 reduce-scatter.1
